TPU v7x, 128 devices: a whole 4x4x4 slice. The times are simulated.
128 devices in a mesh: occ: 8 (over z, core), vir: 16 (over x, y).
Axes of the slice: x: 4, y: 4, z: 4, core: 2. Of those that a mesh axis runs over, the one named last changes fastest.
Arguments:
- amplitudes: bfloat16 [640, 8, 640], P('vir', 'occ'), may hold values from -6 to 6
- tile_list: int32 [8, 5, 1], replicated, may hold values from 0 to 4, as said below
- ladder_factor: bfloat16 [1280, 640, 640], P(('occ', 'vir')), may hold values from -0.0625 to 0.0625
- fock_vv: bfloat16 [640, 640], replicated, may hold values from -0.25 to 0.25
- pair_coupling: float32 [8, 8], replicated, may hold values from -2 to 2
Outputs:
- residual: float32 [640, 8, 640], P('vir', 'occ')
Inputs may be any that keep to these rules, and one draw needn't show every extreme that they name: For each pair p and tile t of a, tile_list[p, t, 0] names the single tile of b that is present.
All inputs are finite; a program needn't handle non-finite values.
Results may differ from a plain program's by a relative error of at most 0.0023.
Values may be sent and summed in bfloat16 or wider, within the bound.
No kernel may reach another device: no remote copies, remote signals or barrier semaphores. Data moves between devices by JAX's collectives and lax.ppermute only.
A program may use at most 128 MiB of HBM per device.

v0:
```python
import jax
import jax.numpy as jnp
from jax import lax
from jax.experimental import pallas as pl
from jax.experimental.pallas import tpu as pltpu
from jax.sharding import Mesh
from jax.sharding import PartitionSpec as P

F32 = jnp.float32
BF16 = jnp.bfloat16
NT = (((1,), (1,)), ((), ()))
TILE = 128
SAME_CORE = ("z", "x", "y")
LADDER_VMEM = 60 << 20
SMALL_VMEM = 8 << 20
AT_ONCE = 4


def place():
    vir = lax.axis_index("x") * lax.axis_size("y") + lax.axis_index("y")
    return lax.axis_index("z") * 2 + lax.axis_index("core"), vir


def row_tiles(vir, rows):
    first = vir * rows
    low = first // TILE
    high = (first + rows - 1) // TILE
    index = lax.broadcasted_iota(jnp.int32, (rows, TILE), 0) + first
    return low, high, index < (low + 1) * TILE


def compact_kernel(lists, amps, out):
    pair, vir = place()
    rows, width = amps.shape
    low, high, in_low = row_tiles(vir, rows)
    chosen = jnp.where(in_low, lists[low, 0, pair], lists[high, 0, pair])
    kept = jnp.zeros((rows, TILE), F32)
    for tile in range(width // TILE):
        part = amps[:, tile * TILE : (tile + 1) * TILE].astype(F32)
        kept = jnp.where(chosen == tile, part, kept)
    out[...] = jnp.broadcast_to(kept.astype(BF16)[None], out.shape)


def ladder_kernel(lists, amps, own, other, out, factor, half, sums, items, sems):
    core = lax.axis_index("core")
    pairs, tiles = amps.shape[0], lists.shape[0]
    depth = own.shape[0]
    width = tiles * TILE

    def copy(source, chunk, tile):
        b_rows = pl.ds(tile * TILE, TILE)
        return pltpu.make_async_copy(source.at[:, b_rows, :], factor.at[chunk, :, b_rows, :], sems.at[chunk, tile])

    for tile in range(tiles):
        copy(own, 0, tile).start()
    count = jnp.int32(0)
    for tile in range(tiles):
        for pair in range(pairs):
            need = lists[0, 0, 2 * pair + core] == tile
            for row in range(1, tiles):
                need = need | (lists[row, 0, 2 * pair + core] == tile)
            items[count] = jnp.int32(pair * 8 + tile)
            count = count + need.astype(jnp.int32)
    sums[...] = jnp.zeros_like(sums)

    def half_of(chunk, index):
        item = items[index]
        pair, tile = item // 8, item % 8
        b_rows = pl.ds(pl.multiple_of(tile * TILE, TILE), TILE)
        for tile_c in range(tiles):
            start = pl.multiple_of(lists[tile_c, 0, 2 * pair + core] * TILE, TILE)
            panel = factor[chunk, :, b_rows, pl.ds(start, TILE)].reshape(depth * TILE, TILE)
            rows = amps[pair, tile_c * TILE : (tile_c + 1) * TILE, :]
            result = lax.dot_general(rows, panel, NT, preferred_element_type=F32).astype(BF16)
            for level in range(depth):
                first = level * width + tile_c * TILE
                half[pair * tiles + tile, first : first + TILE, :] = result[:, level * TILE : (level + 1) * TILE]

    def wait_up_to(chunk, arrived, last):
        for tile in range(tiles):

            @pl.when((arrived <= tile) & (last >= tile))
            def _():
                copy(own, chunk, tile).wait()

        return jnp.maximum(arrived, last + 1)

    def one_chunk(chunk, carry):
        def several(step, arrived):
            first = step * AT_ONCE
            arrived = wait_up_to(chunk, arrived, items[first + AT_ONCE - 1] % 8)
            for index in range(AT_ONCE):
                half_of(chunk, first + index)
            return arrived

        def one(index, carry):
            half_of(chunk, index)
            return carry

        steps = count // AT_ONCE
        arrived = lax.fori_loop(0, steps, several, jnp.int32(0))
        wait_up_to(chunk, arrived, jnp.int32(tiles - 1))
        lax.fori_loop(steps * AT_ONCE, count, one, 0)

        @pl.when(chunk == 0)
        def _():
            for tile in range(tiles):
                copy(other, 1, tile).start()

        for tile_a in range(tiles):
            a_rows = pl.ds(tile_a * TILE, TILE)
            left = jnp.concatenate([factor[chunk, level, a_rows, :] for level in range(depth)], axis=1)
            right = jnp.concatenate(
                [half[pair * tiles + lists[tile_a, 0, 2 * pair + core]] for pair in range(pairs)], axis=1
            )
            result = jnp.dot(left, right, preferred_element_type=F32)
            for pair in range(pairs):
                sums[pair, a_rows, :] += result[:, pair * TILE : (pair + 1) * TILE]
        return carry

    lax.fori_loop(0, 2, one_chunk, 0)
    out[...] = sums[...].astype(BF16)


def local_kernel(lists, coupling, own_side, other_side, amps, fock_rows, fock, out, tile_of_row):
    pair, vir = place()
    core = lax.axis_index("core")
    pairs, rows = own_side.shape[0], own_side.shape[1]
    tiles = lists.shape[0]
    low, high, in_low = row_tiles(vir, rows)
    tile_low, tile_high = lists[low, 0, pair], lists[high, 0, pair]
    total = jnp.zeros((rows, TILE), F32)
    for side, held in ((core, own_side), (1 - core, other_side)):
        for index in range(pairs):
            other = 2 * index + side
            weight = coupling[other, pair]
            none = jnp.float32(0)
            weight_low = jnp.where(lists[low, 0, other] == tile_low, weight, none)
            weight_high = jnp.where(lists[high, 0, other] == tile_high, weight, none)
            total = total + held[index].astype(F32) * jnp.where(in_low, weight_low, weight_high)
    chosen = jnp.where(in_low, tile_low, tile_high)
    masked = []
    for tile_c in range(tiles):
        part = fock_rows[vir, :, tile_c * TILE : (tile_c + 1) * TILE].astype(F32)
        masked.append(jnp.where(chosen == lists[tile_c, 0, pair], part, jnp.zeros_like(part)).astype(BF16))
    left = jnp.concatenate(masked, axis=1)
    total = total + jnp.dot(left, amps[pair // 2], preferred_element_type=F32)
    mine = own_side[pair // 2]
    for tile, keep in ((tile_low, in_low), (tile_high, jnp.logical_not(in_low))):
        span = pl.ds(pl.multiple_of(tile * TILE, TILE), TILE)
        product = lax.dot_general(mine, fock[span, span], NT, preferred_element_type=F32)
        total = total + jnp.where(keep, product, jnp.zeros_like(product))
    out[...] = total
    tile_of_row[...] = chosen


def final_kernel(sums, local, tile_of_row, out):
    chosen = tile_of_row[...]
    total = local[...] + jnp.sum(sums[...].astype(F32), axis=0)
    for tile in range(out.shape[2] // TILE):
        out[:, 0, tile * TILE : (tile + 1) * TILE] = jnp.where(chosen == tile, total, jnp.zeros_like(total))


SMEM = pl.BlockSpec(memory_space=pltpu.SMEM)
VMEM = pl.BlockSpec(memory_space=pltpu.VMEM)
ANY = pl.BlockSpec(memory_space=pl.ANY)


def shards(amplitudes, tile_list, ladder_factor, fock_vv, pair_coupling):
    rows, _, width = amplitudes.shape
    depth = ladder_factor.shape[0]
    pairs = lax.axis_size("z")
    vir_count = lax.axis_size("x") * lax.axis_size("y")
    peers = pairs * vir_count
    swap = [(0, 1), (1, 0)]
    lists = jnp.transpose(tile_list, (1, 2, 0))
    tiles = lists.shape[0]
    _, vir = place()

    other_factor = lax.ppermute(ladder_factor, "core", swap)
    repeated = pl.pallas_call(
        compact_kernel,
        in_specs=[SMEM, VMEM],
        out_specs=VMEM,
        out_shape=jax.ShapeDtypeStruct((peers, rows, TILE), BF16),
        name="compact",
    )(lists, amplitudes.reshape(rows, width))
    gathered = lax.all_to_all(repeated, SAME_CORE, 0, 0, tiled=True)
    amps = gathered.reshape(pairs, width, TILE)

    partial_sums = pl.pallas_call(
        ladder_kernel,
        in_specs=[SMEM, VMEM, ANY, ANY],
        out_specs=VMEM,
        out_shape=jax.ShapeDtypeStruct((pairs, width, TILE), BF16),
        scratch_shapes=[
            pltpu.VMEM((2, depth, width, width), BF16),
            pltpu.VMEM((pairs * tiles, depth * width, TILE), BF16),
            pltpu.VMEM((pairs, width, TILE), F32),
            pltpu.SMEM((pairs * tiles + 1,), jnp.int32),
            pltpu.SemaphoreType.DMA((2, tiles)),
        ],
        compiler_params=pltpu.CompilerParams(vmem_limit_bytes=LADDER_VMEM),
        cost_estimate=pl.CostEstimate(flops=17 * 10**9, bytes_accessed=20 * 10**6, transcendentals=0),
        name="ladder",
    )(lists, amps, ladder_factor, other_factor)

    own_side = lax.dynamic_index_in_dim(gathered.reshape(pairs, vir_count, rows, TILE), vir, 1, keepdims=False)
    other_side = lax.ppermute(own_side, "core", swap)
    local, tile_of_row = pl.pallas_call(
        local_kernel,
        in_specs=[SMEM, SMEM, VMEM, VMEM, VMEM, VMEM, VMEM],
        out_specs=(VMEM, VMEM),
        out_shape=(
            jax.ShapeDtypeStruct((rows, TILE), F32),
            jax.ShapeDtypeStruct((rows, TILE), jnp.int32),
        ),
        compiler_params=pltpu.CompilerParams(vmem_limit_bytes=SMALL_VMEM),
        name="local_terms",
    )(lists, pair_coupling, own_side, other_side, amps, fock_vv.reshape(vir_count, rows, width), fock_vv)

    received = lax.all_to_all(partial_sums.reshape(peers, rows, TILE), SAME_CORE, 0, 0, tiled=True)
    return pl.pallas_call(
        final_kernel,
        in_specs=[VMEM, VMEM, VMEM],
        out_specs=VMEM,
        out_shape=jax.ShapeDtypeStruct((rows, 1, width), F32),
        compiler_params=pltpu.CompilerParams(vmem_limit_bytes=SMALL_VMEM),
        name="final",
    )(received, local, tile_of_row)


def solution(mesh):
    grid = Mesh(mesh.devices.reshape(4, 2, 4, 4), ("z", "core", "x", "y"))
    pairs_of, rows_of = ("z", "core"), ("x", "y")
    in_specs = (P(rows_of, pairs_of, None), P(), P(pairs_of + rows_of, None, None), P(), P())
    out_specs = P(rows_of, pairs_of, None)
    return jax.shard_map(shards, mesh=grid, in_specs=in_specs, out_specs=out_specs, check_vma=False)
```

profile of v0, /device:TPU:0, one launch (start us, length us, event | category | flops | bytes accessed | tf_op | source)
XLA Modules:
  0.0 73.3 jit_solution(7952810720680017803)
XLA Ops:
  0.0 0.0 collective-permute-start
  0.0 1.8 %compact.1 = bf16[64,40,128]{2,1,0:T(8,128)(2,1)} custom-call(s32[5,1,8]{2,1,0:T(1,128)} %bitcast.14, bf16[40,640]{1,0:T(8,128)(2,1)} %bitcast.18), custom_call_target="tpu_custom_call" | custom-call | tf_op jit(solution)/shard_map/compact/pallas_call | solution.py:181
  1.8 26.9 %all_to_all.10 = bf16[64,40,128]{2,1,0:T(8,128)(2,1)} all-to-all(bf16[64,40,128]{2,1,0:T(8,128)(2,1)} %compact.1), channel_id=1, replica_groups=mesh['z'=4,'core'=2,'x'=4,'y'=4] {'z','x','y'}, dimensions={0} | all-to-all | bytes 1310720 | tf_op jit(solution)/shard_map/all_to_all | solution.py:188
  28.7 0.0 collective-permute-done.other
  28.7 0.0 copy-start.1
  28.7 0.0 copy-start
  28.7 0.0 copy-start.2
  28.7 0.0 copy-start.3
  28.7 26.3 %ladder.1 = bf16[4,640,128]{2,1,0:T(8,128)(2,1)} custom-call(s32[5,1,8]{2,1,0:T(1,128)} %bitcast.15, bf16[4,640,128]{2,1,0:T(8,128)(2,1)} %bitcast.11, bf16[10,640,640]{2,1,0:T(8,128)(2,1)} %own.1, bf16[10,640,640]{2,1,0:T(8,128)(2,1)} %collective-permute-done.other), custom_call_target="tpu_custom_call" | custom-call | flops 16999999488 | bytes 20000000 | tf_op jit(solution)/shard_map/ladder/pallas_call | solution.py:191
  55.1 4.8 %all-to-all-start.1 = ((bf16[64,40,128]{2,1,0:T(8,128)(2,1)}), bf16[64,40,128]{2,1,0:T(8,128)(2,1)S(1)}, u32[]{:S(2)}, u32[]{:S(2)}) async-start(bf16[64,40,128]{2,1,0:T(8,128)(2,1)} %bitcast.17), calls=%async_computation.1 | async-start | bytes 1310720 | tf_op jit(solution)/shard_map/all_to_all | solution.py:222
  59.9 0.0 copy-done.1
  59.9 0.1 collective-permute-start.1
  60.0 1.2 %collective-permute-done.1.other_side = bf16[4,40,128]{2,1,0:T(8,128)(2,1)S(1)} collective-permute-done((bf16[4,40,128]{2,1,0:T(8,128)(2,1)S(1)}, bf16[4,40,128]{2,1,0:T(8,128)(2,1)S(1)}, u32[]{:S(2)}, u32[]{:S(2)}) %collective-permute-start.1) | collective-permute-done | bytes 40992 | tf_op jit(solution)/shard_map/ppermute | solution.py:209
  61.2 0.0 copy-done
  61.2 0.0 copy-done.2
  61.2 0.0 copy-done.3
  61.2 0.9 %local_terms.1 = (f32[40,128]{1,0:T(8,128)S(1)}, s32[40,128]{1,0:T(8,128)S(1)}) custom-call(s32[5,1,8]{2,1,0:T(1,128)S(1)} %bitcast.16, f32[8,8]{1,0:T(8,128)S(1)} %copy-done.3, bf16[4,40,128]{2,1,0:T(8,128)(2,1)S(1)} %dynamic-slice_bitcast_fusion.own_side, bf16[4,40,128]{2,1,0:T(8,128)(2,1)S(1)} %collective-permute-done.1.other_side, ...), custom_call_target="tpu_custom_call" | custom-call | tf_op jit(solution)/shard_map/local_terms/pallas_call | solution.py:210
  62.1 10.4 %all-to-all-done.1.sums = bf16[64,40,128]{2,1,0:T(8,128)(2,1)S(1)} async-done(((bf16[64,40,128]{2,1,0:T(8,128)(2,1)}), bf16[64,40,128]{2,1,0:T(8,128)(2,1)S(1)}, u32[]{:S(2)}, u32[]{:S(2)}) %all-to-all-start.1) | async-done | bytes 655392 | tf_op jit(solution)/shard_map/all_to_all | solution.py:222
  72.5 0.8 %final.1 = f32[40,1,640]{2,1,0:T(1,128)} custom-call(bf16[64,40,128]{2,1,0:T(8,128)(2,1)S(1)} %all-to-all-done.1.sums, f32[40,128]{1,0:T(8,128)S(1)} %get-tuple-element.7.local, s32[40,128]{1,0:T(8,128)S(1)} %get-tuple-element.8.tile_of_row), custom_call_target="tpu_custom_call" | custom-call | tf_op jit(solution)/shard_map/final/pallas_call | solution.py:223
  (1 shorter events, 0.0 us)
Async XLA Ops:
  0.0 28.7 %collective-permute-start = (bf16[10,640,640]{2,1,0:T(8,128)(2,1)}, bf16[10,640,640]{2,1,0:T(8,128)(2,1)}, u32[]{:S(2)}, u32[]{:S(2)}) collective-permute-start(bf16[10,640,640]{2,1,0:T(8,128)(2,1)} %own.1), channel_id=1, source_target_pairs={{0,16},{16,0},{1,17},{17,1},{2,18},{18,2},{3,19},{19,3},{4,20},{20... | collective-permute-start | bytes 24576008 | tf_op jit(solution)/shard_map/ppermute | solution.py:180
  28.7 31.2 %copy-start.1 = (bf16[64,40,128]{2,1,0:T(8,128)(2,1)S(1)}, bf16[64,40,128]{2,1,0:T(8,128)(2,1)}, u32[]{:S(2)}) copy-start(bf16[64,40,128]{2,1,0:T(8,128)(2,1)} %all_to_all.10) | copy-start | bytes 1966084
  28.7 32.5 %copy-start = (bf16[640,640]{1,0:T(8,128)(2,1)S(1)}, bf16[640,640]{1,0:T(8,128)(2,1)}, u32[]{:S(2)}) copy-start(bf16[640,640]{1,0:T(8,128)(2,1)} %fock.1) | copy-start | bytes 2457604
  28.7 32.5 %copy-start.2 = (s32[8,5,1]{0,2,1:T(1,128)S(1)}, s32[8,5,1]{0,2,1:T(1,128)}, u32[]{:S(2)}) copy-start(s32[8,5,1]{0,2,1:T(1,128)} %param.6) | copy-start | bytes 484
  28.7 32.5 %copy-start.3 = (f32[8,8]{1,0:T(8,128)S(1)}, f32[8,8]{1,0:T(8,128)}, u32[]{:S(2)}) copy-start(f32[8,8]{1,0:T(8,128)} %coupling.1) | copy-start | bytes 772
  55.1 17.4 %all-to-all-start.1 = ((bf16[64,40,128]{2,1,0:T(8,128)(2,1)}), bf16[64,40,128]{2,1,0:T(8,128)(2,1)S(1)}, u32[]{:S(2)}, u32[]{:S(2)}) async-start(bf16[64,40,128]{2,1,0:T(8,128)(2,1)} %bitcast.17), calls=%async_computation.1 | async-start | bytes 1310720 | tf_op jit(solution)/shard_map/all_to_all | solution.py:222
  59.9 1.3 %collective-permute-start.1 = (bf16[4,40,128]{2,1,0:T(8,128)(2,1)S(1)}, bf16[4,40,128]{2,1,0:T(8,128)(2,1)S(1)}, u32[]{:S(2)}, u32[]{:S(2)}) collective-permute-start(bf16[4,40,128]{2,1,0:T(8,128)(2,1)S(1)} %dynamic-slice_bitcast_fusion.own_side), channel_id=1, source_target_pairs={{0,16},{16,0},{1,17},{17,1},{2,18},{18,2},{3,19},{19,3},{4,20},{20... | collective-permute-start | bytes 122888 | tf_op jit(solution)/shard_map/ppermute | solution.py:209
where the time goes:
time: 73.3 us
  Pallas kernels  29.8 us (41%)
  blocking collectives  26.9 us (37%)
  waiting for transfers between devices  11.6 us (16%)
  starting transfers between devices  4.87 us (7%)
    all_to_all x1, blocking collectives, shards(): gathered = lax.all_to_all(repeated, SAME_CORE, 0, 0, tiled=True)  26.9 us
    pallas_call x1, Pallas kernels, shards(): pl.pallas_call(ladder_kernel, in_specs=[SMEM, VMEM, ANY, ANY], out_specs=...  26.3 us
    all_to_all x1, waiting for transfers between devices, shards(): lax.all_to_all(partial_sums.reshape(peers, rows, TILE), SAME_CORE, 0, 0,...  10.4 us
    all_to_all x1, starting transfers between devices, shards(): lax.all_to_all(partial_sums.reshape(peers, rows, TILE), SAME_CORE, 0, 0,...  4.78 us
    pallas_call x1, Pallas kernels, shards(): pl.pallas_call(compact_kernel, in_specs=[SMEM, VMEM], out_specs=VMEM, out...  1.77 us
  transfers between devices with their start and end apart: 3, of which 2 were waited for; matrix products, arithmetic and copies ran while one was open for 0% of the time, Pallas kernels for 4%

commit v1 on v0

--- a/solution.py
+++ b/solution.py
@@ -11,8 +11,9 @@
 NT = (((1,), (1,)), ((), ()))
 TILE = 128
 SAME_CORE = ("z", "x", "y")
-LADDER_VMEM = 60 << 20
+LADDER_VMEM = 57 << 20
 SMALL_VMEM = 8 << 20
+COMPACT_VMEM = 57 << 20
 AT_ONCE = 4
 
 
@@ -166,6 +167,14 @@
 ANY = pl.BlockSpec(memory_space=pl.ANY)
 
 
+def in_hbm(array):
+    return pltpu.with_memory_space_constraint(array, pltpu.HBM)
+
+
+def in_vmem(array):
+    return pltpu.with_memory_space_constraint(array, pltpu.VMEM)
+
+
 def shards(amplitudes, tile_list, ladder_factor, fock_vv, pair_coupling):
     rows, _, width = amplitudes.shape
     depth = ladder_factor.shape[0]
@@ -182,9 +191,10 @@
         compact_kernel,
         in_specs=[SMEM, VMEM],
         out_specs=VMEM,
-        out_shape=jax.ShapeDtypeStruct((peers, rows, TILE), BF16),
+        out_shape=pltpu.VMEM((peers, rows, TILE), BF16),
+        compiler_params=pltpu.CompilerParams(vmem_limit_bytes=COMPACT_VMEM),
         name="compact",
-    )(lists, amplitudes.reshape(rows, width))
+    )(in_hbm(lists), in_hbm(amplitudes.reshape(rows, width)))
     gathered = lax.all_to_all(repeated, SAME_CORE, 0, 0, tiled=True)
     amps = gathered.reshape(pairs, width, TILE)
 
@@ -192,7 +202,7 @@
         ladder_kernel,
         in_specs=[SMEM, VMEM, ANY, ANY],
         out_specs=VMEM,
-        out_shape=jax.ShapeDtypeStruct((pairs, width, TILE), BF16),
+        out_shape=pltpu.VMEM((pairs, width, TILE), BF16),
         scratch_shapes=[
             pltpu.VMEM((2, depth, width, width), BF16),
             pltpu.VMEM((pairs * tiles, depth * width, TILE), BF16),
@@ -203,7 +213,7 @@
         compiler_params=pltpu.CompilerParams(vmem_limit_bytes=LADDER_VMEM),
         cost_estimate=pl.CostEstimate(flops=17 * 10**9, bytes_accessed=20 * 10**6, transcendentals=0),
         name="ladder",
-    )(lists, amps, ladder_factor, other_factor)
+    )(in_hbm(lists), in_vmem(amps), in_hbm(ladder_factor), in_hbm(other_factor))
 
     own_side = lax.dynamic_index_in_dim(gathered.reshape(pairs, vir_count, rows, TILE), vir, 1, keepdims=False)
     other_side = lax.ppermute(own_side, "core", swap)

time: 73.3 us -> 75 us (1.023)
  waiting for transfers between devices: 11.6 us -> 14.1 us
  Pallas kernels: 29.8 us -> 28.5 us
    all_to_all x1, waiting for transfers between devices: 10.4 us -> 13.2 us  [shards(): lax.all_to_all(partial_sums.reshape(peers, rows, TILE), SAME_CORE, 0, 0,...]
    pallas_call x1, Pallas kernels: 1.77 us -> 0.89 us  [shards(): pl.pallas_call(compact_kernel, in_specs=[SMEM, VMEM], out_specs=VMEM, out...]
  transfers between devices with their start and end apart: 3 -> 3, of which waited for: 2 -> 2; matrix products, arithmetic and copies ran while one was open for 0% -> 0% of each run, Pallas kernels for 4% -> 2%
where the time goes in v1:
time: 75 us; the launch traced here: 74.7 us
  Pallas kernels  28.5 us (38%)
  blocking collectives  26.6 us (35%)
  waiting for transfers between devices  14.1 us (19%)
  starting transfers between devices  5.34 us (7%)
    all_to_all x1, blocking collectives, shards(): gathered = lax.all_to_all(repeated, SAME_CORE, 0, 0, tiled=True)  26.6 us
    pallas_call x1, Pallas kernels, shards(): pl.pallas_call(ladder_kernel, in_specs=[SMEM, VMEM, ANY, ANY], out_specs=...  26 us
    all_to_all x1, waiting for transfers between devices, shards(): lax.all_to_all(partial_sums.reshape(peers, rows, TILE), SAME_CORE, 0, 0,...  13.2 us
    all_to_all x1, starting transfers between devices, shards(): lax.all_to_all(partial_sums.reshape(peers, rows, TILE), SAME_CORE, 0, 0,...  4.78 us
  transfers between devices with their start and end apart: 3, of which 2 were waited for; matrix products, arithmetic and copies ran while one was open for 0% of the time, Pallas kernels for 2%

profile of v1, /device:TPU:0, one launch (start us, length us, event | category | flops | bytes accessed | tf_op | source)
XLA Modules:
  0.0 74.7 jit_solution(10515322950515731404)
XLA Ops:
  0.0 0.0 collective-permute-start
  0.0 0.9 %compact.1 = bf16[64,40,128]{2,1,0:T(8,128)(2,1)S(1)} custom-call(s32[5,1,8]{2,1,0:T(1,128)} %bitcast.14, bf16[40,640]{1,0:T(8,128)(2,1)} %bitcast.17), custom_call_target="tpu_custom_call" | custom-call | tf_op jit(solution)/shard_map/compact/pallas_call | solution.py:190
  0.9 26.6 %all_to_all.10 = bf16[64,40,128]{2,1,0:T(8,128)(2,1)S(1)} all-to-all(bf16[64,40,128]{2,1,0:T(8,128)(2,1)S(1)} %compact.1), channel_id=1, replica_groups=mesh['z'=4,'core'=2,'x'=4,'y'=4] {'z','x','y'}, dimensions={0} | all-to-all | bytes 1310720 | tf_op jit(solution)/shard_map/all_to_all | solution.py:198
  27.5 0.0 collective-permute-done.other
  27.5 0.0 copy-start
  27.5 0.0 copy-start.1
  27.5 0.0 copy-start.2
  27.5 26.0 %ladder.1 = bf16[4,640,128]{2,1,0:T(8,128)(2,1)} custom-call(s32[5,1,8]{2,1,0:T(1,128)} %bitcast.15, bf16[4,640,128]{2,1,0:T(8,128)(2,1)S(1)} %bitcast.11, bf16[10,640,640]{2,1,0:T(8,128)(2,1)} %own.1, bf16[10,640,640]{2,1,0:T(8,128)(2,1)} %collective-permute-done.other), custom_call_target="tpu_custom_call" | custom-call | flops 16999999488 | bytes 20000000 | tf_op jit(solution)/shard_map/ladder/pallas_call | solution.py:201
  53.5 4.8 %all-to-all-start.1 = ((bf16[64,40,128]{2,1,0:T(8,128)(2,1)}), bf16[64,40,128]{2,1,0:T(8,128)(2,1)S(1)}, u32[]{:S(2)}, u32[]{:S(2)}) async-start(bf16[64,40,128]{2,1,0:T(8,128)(2,1)} %bitcast.3), calls=%async_computation.1 | async-start | bytes 1310720 | tf_op jit(solution)/shard_map/all_to_all | solution.py:232
  58.3 0.6 collective-permute-start.1
  58.9 0.9 %collective-permute-done.1.other_side = bf16[4,40,128]{2,1,0:T(8,128)(2,1)S(1)} collective-permute-done((bf16[4,40,128]{2,1,0:T(8,128)(2,1)S(1)}, bf16[4,40,128]{2,1,0:T(8,128)(2,1)S(1)}, u32[]{:S(2)}, u32[]{:S(2)}) %collective-permute-start.1) | collective-permute-done | bytes 40992 | tf_op jit(solution)/shard_map/ppermute | solution.py:219
  59.7 0.0 copy-done
  59.7 0.0 copy-done.1
  59.7 0.0 copy-done.2
  59.7 0.9 %local_terms.1 = (f32[40,128]{1,0:T(8,128)S(1)}, s32[40,128]{1,0:T(8,128)S(1)}) custom-call(s32[5,1,8]{2,1,0:T(1,128)S(1)} %bitcast.16, f32[8,8]{1,0:T(8,128)S(1)} %copy-done.2, bf16[4,40,128]{2,1,0:T(8,128)(2,1)S(1)} %dynamic-slice_bitcast_fusion.own_side, bf16[4,40,128]{2,1,0:T(8,128)(2,1)S(1)} %collective-permute-done.1.other_side, ...), custom_call_target="tpu_custom_call" | custom-call | tf_op jit(solution)/shard_map/local_terms/pallas_call | solution.py:220
  60.6 13.2 %all-to-all-done.1.sums = bf16[64,40,128]{2,1,0:T(8,128)(2,1)S(1)} async-done(((bf16[64,40,128]{2,1,0:T(8,128)(2,1)}), bf16[64,40,128]{2,1,0:T(8,128)(2,1)S(1)}, u32[]{:S(2)}, u32[]{:S(2)}) %all-to-all-start.1) | async-done | bytes 655392 | tf_op jit(solution)/shard_map/all_to_all | solution.py:232
  73.8 0.8 %final.1 = f32[40,1,640]{2,1,0:T(1,128)} custom-call(bf16[64,40,128]{2,1,0:T(8,128)(2,1)S(1)} %all-to-all-done.1.sums, f32[40,128]{1,0:T(8,128)S(1)} %get-tuple-element.7.local, s32[40,128]{1,0:T(8,128)S(1)} %get-tuple-element.8.tile_of_row), custom_call_target="tpu_custom_call" | custom-call | tf_op jit(solution)/shard_map/final/pallas_call | solution.py:233
  (1 shorter events, 0.0 us)
Async XLA Ops:
  0.0 27.5 %collective-permute-start = (bf16[10,640,640]{2,1,0:T(8,128)(2,1)}, bf16[10,640,640]{2,1,0:T(8,128)(2,1)}, u32[]{:S(2)}, u32[]{:S(2)}) collective-permute-start(bf16[10,640,640]{2,1,0:T(8,128)(2,1)} %own.1), channel_id=1, source_target_pairs={{0,16},{16,0},{1,17},{17,1},{2,18},{18,2},{3,19},{19,3},{4,20},{20... | collective-permute-start | bytes 24576008 | tf_op jit(solution)/shard_map/ppermute | solution.py:189
  27.5 32.2 %copy-start = (bf16[640,640]{1,0:T(8,128)(2,1)S(1)}, bf16[640,640]{1,0:T(8,128)(2,1)}, u32[]{:S(2)}) copy-start(bf16[640,640]{1,0:T(8,128)(2,1)} %fock.1) | copy-start | bytes 2457604
  27.5 32.2 %copy-start.1 = (s32[8,5,1]{0,2,1:T(1,128)S(1)}, s32[8,5,1]{0,2,1:T(1,128)}, u32[]{:S(2)}) copy-start(s32[8,5,1]{0,2,1:T(1,128)} %param.6) | copy-start | bytes 484
  27.5 32.2 %copy-start.2 = (f32[8,8]{1,0:T(8,128)S(1)}, f32[8,8]{1,0:T(8,128)}, u32[]{:S(2)}) copy-start(f32[8,8]{1,0:T(8,128)} %coupling.1) | copy-start | bytes 772
  53.5 20.3 %all-to-all-start.1 = ((bf16[64,40,128]{2,1,0:T(8,128)(2,1)}), bf16[64,40,128]{2,1,0:T(8,128)(2,1)S(1)}, u32[]{:S(2)}, u32[]{:S(2)}) async-start(bf16[64,40,128]{2,1,0:T(8,128)(2,1)} %bitcast.3), calls=%async_computation.1 | async-start | bytes 1310720 | tf_op jit(solution)/shard_map/all_to_all | solution.py:232
  58.3 1.4 %collective-permute-start.1 = (bf16[4,40,128]{2,1,0:T(8,128)(2,1)S(1)}, bf16[4,40,128]{2,1,0:T(8,128)(2,1)S(1)}, u32[]{:S(2)}, u32[]{:S(2)}) collective-permute-start(bf16[4,40,128]{2,1,0:T(8,128)(2,1)S(1)} %dynamic-slice_bitcast_fusion.own_side), channel_id=1, source_target_pairs={{0,16},{16,0},{1,17},{17,1},{2,18},{18,2},{3,19},{19,3},{4,20},{20... | collective-permute-start | bytes 122888 | tf_op jit(solution)/shard_map/ppermute | solution.py:219

commit v2 on v1

--- a/solution.py
+++ b/solution.py
@@ -14,7 +14,7 @@
 LADDER_VMEM = 57 << 20
 SMALL_VMEM = 8 << 20
 COMPACT_VMEM = 57 << 20
-AT_ONCE = 4
+AT_ONCE = 8
 
 
 def place():
@@ -87,21 +87,29 @@
         return jnp.maximum(arrived, last + 1)
 
     def one_chunk(chunk, carry):
-        def several(step, arrived):
-            first = step * AT_ONCE
-            arrived = wait_up_to(chunk, arrived, items[first + AT_ONCE - 1] % 8)
-            for index in range(AT_ONCE):
+        def several(first, size, arrived):
+            arrived = wait_up_to(chunk, arrived, items[first + size - 1] % 8)
+            for index in range(size):
                 half_of(chunk, first + index)
             return arrived
 
-        def one(index, carry):
-            half_of(chunk, index)
-            return carry
-
-        steps = count // AT_ONCE
-        arrived = lax.fori_loop(0, steps, several, jnp.int32(0))
+        first, arrived, size = jnp.int32(0), jnp.int32(0), 1
+        while size < AT_ONCE:
+            odd = (count // size) % 2 == 1
+            last = jnp.where(odd, items[jnp.minimum(first + size, count) - 1] % 8, -1)
+            arrived = wait_up_to(chunk, arrived, last)
+
+            @pl.when(odd)
+            def _():
+                for index in range(size):
+                    half_of(chunk, first + index)
+
+            first = jnp.where(odd, first + size, first)
+            size *= 2
+        arrived = lax.fori_loop(
+            0, count // AT_ONCE, lambda step, seen: several(first + step * AT_ONCE, AT_ONCE, seen), arrived
+        )
         wait_up_to(chunk, arrived, jnp.int32(tiles - 1))
-        lax.fori_loop(steps * AT_ONCE, count, one, 0)
 
         @pl.when(chunk == 0)
         def _():

time: 75 us -> 71.3 us (0.951)
  Pallas kernels: 28.5 us -> 24.9 us
    pallas_call x1, Pallas kernels: 26 us -> 22.4 us  [shards(): pl.pallas_call(ladder_kernel, in_specs=[SMEM, VMEM, ANY, ANY], out_specs=...]
where the time goes in v2:
time: 71.3 us; the launch traced here: 70.7 us
  blocking collectives  26.6 us (37%)
  Pallas kernels  24.9 us (35%)
  waiting for transfers between devices  14.1 us (20%)
  starting transfers between devices  4.96 us (7%)
    all_to_all x1, blocking collectives, shards(): gathered = lax.all_to_all(repeated, SAME_CORE, 0, 0, tiled=True)  26.6 us
    pallas_call x1, Pallas kernels, shards(): pl.pallas_call(ladder_kernel, in_specs=[SMEM, VMEM, ANY, ANY], out_specs=...  22.4 us
    all_to_all x1, waiting for transfers between devices, shards(): lax.all_to_all(partial_sums.reshape(peers, rows, TILE), SAME_CORE, 0, 0,...  13 us
    all_to_all x1, starting transfers between devices, shards(): lax.all_to_all(partial_sums.reshape(peers, rows, TILE), SAME_CORE, 0, 0,...  4.78 us
  transfers between devices with their start and end apart: 3, of which 2 were waited for; matrix products, arithmetic and copies ran while one was open for 0% of the time, Pallas kernels for 2%

profile of v2, /device:TPU:0, one launch (start us, length us, event | category | flops | bytes accessed | tf_op | source)
XLA Modules:
  0.0 70.7 jit_solution(12217371712405497441)
XLA Ops:
  0.0 0.0 collective-permute-start
  0.0 0.9 %compact.1 = bf16[64,40,128]{2,1,0:T(8,128)(2,1)S(1)} custom-call(s32[5,1,8]{2,1,0:T(1,128)} %bitcast.14, bf16[40,640]{1,0:T(8,128)(2,1)} %bitcast.17), custom_call_target="tpu_custom_call" | custom-call | tf_op jit(solution)/shard_map/compact/pallas_call | solution.py:198
  0.9 26.6 %all_to_all.10 = bf16[64,40,128]{2,1,0:T(8,128)(2,1)S(1)} all-to-all(bf16[64,40,128]{2,1,0:T(8,128)(2,1)S(1)} %compact.1), channel_id=1, replica_groups=mesh['z'=4,'core'=2,'x'=4,'y'=4] {'z','x','y'}, dimensions={0} | all-to-all | bytes 1310720 | tf_op jit(solution)/shard_map/all_to_all | solution.py:206
  27.5 0.0 collective-permute-done.other
  27.5 0.0 copy-start
  27.5 0.0 copy-start.1
  27.5 0.0 copy-start.2
  27.5 22.4 %ladder.1 = bf16[4,640,128]{2,1,0:T(8,128)(2,1)} custom-call(s32[5,1,8]{2,1,0:T(1,128)} %bitcast.15, bf16[4,640,128]{2,1,0:T(8,128)(2,1)S(1)} %bitcast.11, bf16[10,640,640]{2,1,0:T(8,128)(2,1)} %own.1, bf16[10,640,640]{2,1,0:T(8,128)(2,1)} %collective-permute-done.other), custom_call_target="tpu_custom_call" | custom-call | flops 16999999488 | bytes 20000000 | tf_op jit(solution)/shard_map/ladder/pallas_call | solution.py:209
  49.9 4.8 %all-to-all-start.1 = ((bf16[64,40,128]{2,1,0:T(8,128)(2,1)}), bf16[64,40,128]{2,1,0:T(8,128)(2,1)S(1)}, u32[]{:S(2)}, u32[]{:S(2)}) async-start(bf16[64,40,128]{2,1,0:T(8,128)(2,1)} %bitcast.3), calls=%async_computation.1 | async-start | bytes 1310720 | tf_op jit(solution)/shard_map/all_to_all | solution.py:240
  54.7 0.2 collective-permute-start.1
  54.9 1.1 %collective-permute-done.1.other_side = bf16[4,40,128]{2,1,0:T(8,128)(2,1)S(1)} collective-permute-done((bf16[4,40,128]{2,1,0:T(8,128)(2,1)S(1)}, bf16[4,40,128]{2,1,0:T(8,128)(2,1)S(1)}, u32[]{:S(2)}, u32[]{:S(2)}) %collective-permute-start.1) | collective-permute-done | bytes 40992 | tf_op jit(solution)/shard_map/ppermute | solution.py:227
  56.0 0.0 copy-done
  56.0 0.0 copy-done.1
  56.0 0.0 copy-done.2
  56.0 0.9 %local_terms.1 = (f32[40,128]{1,0:T(8,128)S(1)}, s32[40,128]{1,0:T(8,128)S(1)}) custom-call(s32[5,1,8]{2,1,0:T(1,128)S(1)} %bitcast.16, f32[8,8]{1,0:T(8,128)S(1)} %copy-done.2, bf16[4,40,128]{2,1,0:T(8,128)(2,1)S(1)} %dynamic-slice_bitcast_fusion.own_side, bf16[4,40,128]{2,1,0:T(8,128)(2,1)S(1)} %collective-permute-done.1.other_side, ...), custom_call_target="tpu_custom_call" | custom-call | tf_op jit(solution)/shard_map/local_terms/pallas_call | solution.py:228
  56.9 13.0 %all-to-all-done.1.sums = bf16[64,40,128]{2,1,0:T(8,128)(2,1)S(1)} async-done(((bf16[64,40,128]{2,1,0:T(8,128)(2,1)}), bf16[64,40,128]{2,1,0:T(8,128)(2,1)S(1)}, u32[]{:S(2)}, u32[]{:S(2)}) %all-to-all-start.1) | async-done | bytes 655392 | tf_op jit(solution)/shard_map/all_to_all | solution.py:240
  69.9 0.8 %final.1 = f32[40,1,640]{2,1,0:T(1,128)} custom-call(bf16[64,40,128]{2,1,0:T(8,128)(2,1)S(1)} %all-to-all-done.1.sums, f32[40,128]{1,0:T(8,128)S(1)} %get-tuple-element.7.local, s32[40,128]{1,0:T(8,128)S(1)} %get-tuple-element.8.tile_of_row), custom_call_target="tpu_custom_call" | custom-call | tf_op jit(solution)/shard_map/final/pallas_call | solution.py:241
  (1 shorter events, 0.0 us)
Async XLA Ops:
  0.0 27.5 %collective-permute-start = (bf16[10,640,640]{2,1,0:T(8,128)(2,1)}, bf16[10,640,640]{2,1,0:T(8,128)(2,1)}, u32[]{:S(2)}, u32[]{:S(2)}) collective-permute-start(bf16[10,640,640]{2,1,0:T(8,128)(2,1)} %own.1), channel_id=1, source_target_pairs={{0,16},{16,0},{1,17},{17,1},{2,18},{18,2},{3,19},{19,3},{4,20},{20... | collective-permute-start | bytes 24576008 | tf_op jit(solution)/shard_map/ppermute | solution.py:197
  27.5 28.5 %copy-start = (bf16[640,640]{1,0:T(8,128)(2,1)S(1)}, bf16[640,640]{1,0:T(8,128)(2,1)}, u32[]{:S(2)}) copy-start(bf16[640,640]{1,0:T(8,128)(2,1)} %fock.1) | copy-start | bytes 2457604
  27.5 28.5 %copy-start.1 = (s32[8,5,1]{0,2,1:T(1,128)S(1)}, s32[8,5,1]{0,2,1:T(1,128)}, u32[]{:S(2)}) copy-start(s32[8,5,1]{0,2,1:T(1,128)} %param.6) | copy-start | bytes 484
  27.5 28.5 %copy-start.2 = (f32[8,8]{1,0:T(8,128)S(1)}, f32[8,8]{1,0:T(8,128)}, u32[]{:S(2)}) copy-start(f32[8,8]{1,0:T(8,128)} %coupling.1) | copy-start | bytes 772
  49.9 20.0 %all-to-all-start.1 = ((bf16[64,40,128]{2,1,0:T(8,128)(2,1)}), bf16[64,40,128]{2,1,0:T(8,128)(2,1)S(1)}, u32[]{:S(2)}, u32[]{:S(2)}) async-start(bf16[64,40,128]{2,1,0:T(8,128)(2,1)} %bitcast.3), calls=%async_computation.1 | async-start | bytes 1310720 | tf_op jit(solution)/shard_map/all_to_all | solution.py:240
  54.7 1.3 %collective-permute-start.1 = (bf16[4,40,128]{2,1,0:T(8,128)(2,1)S(1)}, bf16[4,40,128]{2,1,0:T(8,128)(2,1)S(1)}, u32[]{:S(2)}, u32[]{:S(2)}) collective-permute-start(bf16[4,40,128]{2,1,0:T(8,128)(2,1)S(1)} %dynamic-slice_bitcast_fusion.own_side), channel_id=1, source_target_pairs={{0,16},{16,0},{1,17},{17,1},{2,18},{18,2},{3,19},{19,3},{4,20},{20... | collective-permute-start | bytes 122888 | tf_op jit(solution)/shard_map/ppermute | solution.py:227

commit v3 on v2

--- a/solution.py
+++ b/solution.py
@@ -42,18 +42,22 @@
     out[...] = jnp.broadcast_to(kept.astype(BF16)[None], out.shape)
 
 
-def ladder_kernel(lists, amps, own, other, out, factor, half, sums, items, sems):
+def ladder_kernel(lists_in, amps, own, other, out, lists, factor, half, sums, items, sems, list_sem):
     core = lax.axis_index("core")
     pairs, tiles = amps.shape[0], lists.shape[0]
     depth = own.shape[0]
     width = tiles * TILE
 
     def copy(source, chunk, tile):
-        b_rows = pl.ds(tile * TILE, TILE)
+        b_rows = pl.ds(pl.multiple_of(tile * TILE, TILE), TILE)
         return pltpu.make_async_copy(source.at[:, b_rows, :], factor.at[chunk, :, b_rows, :], sems.at[chunk, tile])
 
     for tile in range(tiles):
         copy(own, 0, tile).start()
+        if tile == 0:
+            list_copy = pltpu.make_async_copy(lists_in, lists, list_sem)
+            list_copy.start()
+    list_copy.wait()
     count = jnp.int32(0)
     for tile in range(tiles):
         for pair in range(pairs):
@@ -78,12 +82,11 @@
                 half[pair * tiles + tile, first : first + TILE, :] = result[:, level * TILE : (level + 1) * TILE]
 
     def wait_up_to(chunk, arrived, last):
-        for tile in range(tiles):
-
-            @pl.when((arrived <= tile) & (last >= tile))
-            def _():
-                copy(own, chunk, tile).wait()
-
+        def one(tile, carry):
+            copy(own, chunk, tile).wait()
+            return carry
+
+        lax.fori_loop(arrived, last + 1, one, 0)
         return jnp.maximum(arrived, last + 1)
 
     def one_chunk(chunk, carry):
@@ -208,15 +211,17 @@
 
     partial_sums = pl.pallas_call(
         ladder_kernel,
-        in_specs=[SMEM, VMEM, ANY, ANY],
+        in_specs=[ANY, VMEM, ANY, ANY],
         out_specs=VMEM,
         out_shape=pltpu.VMEM((pairs, width, TILE), BF16),
         scratch_shapes=[
+            pltpu.SMEM(lists.shape, jnp.int32),
             pltpu.VMEM((2, depth, width, width), BF16),
             pltpu.VMEM((pairs * tiles, depth * width, TILE), BF16),
             pltpu.VMEM((pairs, width, TILE), F32),
             pltpu.SMEM((pairs * tiles + 1,), jnp.int32),
             pltpu.SemaphoreType.DMA((2, tiles)),
+            pltpu.SemaphoreType.DMA,
         ],
         compiler_params=pltpu.CompilerParams(vmem_limit_bytes=LADDER_VMEM),
         cost_estimate=pl.CostEstimate(flops=17 * 10**9, bytes_accessed=20 * 10**6, transcendentals=0),

time: 71.3 us -> 71.5 us (level); the launches traced: 70.7 us -> 72.5 us
  Pallas kernels: 24.9 us -> 29.4 us
  waiting for transfers between devices: 14.1 us -> 11.5 us
    pallas_call x1, Pallas kernels: 22.4 us -> 26.9 us  [shards(): pl.pallas_call(ladder_kernel, in_specs=[ANY, VMEM, ANY, ANY], out_specs=V...]
    all_to_all x1, waiting for transfers between devices: 13 us -> 10.3 us  [shards(): lax.all_to_all(partial_sums.reshape(peers, rows, TILE), SAME_CORE, 0, 0,...]
where the time goes in v3:
time: 71.5 us; the launch traced here: 72.5 us
  Pallas kernels  29.4 us (41%)
  blocking collectives  26.6 us (37%)
  waiting for transfers between devices  11.5 us (16%)
  starting transfers between devices  4.87 us (7%)
    pallas_call x1, Pallas kernels, shards(): pl.pallas_call(ladder_kernel, in_specs=[ANY, VMEM, ANY, ANY], out_specs=V...  26.9 us
    all_to_all x1, blocking collectives, shards(): gathered = lax.all_to_all(repeated, SAME_CORE, 0, 0, tiled=True)  26.6 us
    all_to_all x1, waiting for transfers between devices, shards(): lax.all_to_all(partial_sums.reshape(peers, rows, TILE), SAME_CORE, 0, 0,...  10.3 us
    all_to_all x1, starting transfers between devices, shards(): lax.all_to_all(partial_sums.reshape(peers, rows, TILE), SAME_CORE, 0, 0,...  4.78 us
  transfers between devices with their start and end apart: 3, of which 2 were waited for; matrix products, arithmetic and copies ran while one was open for 0% of the time, Pallas kernels for 2%

profile of v3, /device:TPU:0, one launch (start us, length us, event | category | flops | bytes accessed | tf_op | source)
XLA Modules:
  0.0 72.5 jit_solution(4892739441025068900)
XLA Ops:
  0.0 0.0 collective-permute-start
  0.0 0.9 %compact.1 = bf16[64,40,128]{2,1,0:T(8,128)(2,1)S(1)} custom-call(s32[5,1,8]{2,1,0:T(1,128)} %bitcast.14, bf16[40,640]{1,0:T(8,128)(2,1)} %bitcast.17), custom_call_target="tpu_custom_call" | custom-call | tf_op jit(solution)/shard_map/compact/pallas_call | solution.py:201
  0.9 26.6 %all_to_all.10 = bf16[64,40,128]{2,1,0:T(8,128)(2,1)S(1)} all-to-all(bf16[64,40,128]{2,1,0:T(8,128)(2,1)S(1)} %compact.1), channel_id=1, replica_groups=mesh['z'=4,'core'=2,'x'=4,'y'=4] {'z','x','y'}, dimensions={0} | all-to-all | bytes 1310720 | tf_op jit(solution)/shard_map/all_to_all | solution.py:209
  27.5 0.0 collective-permute-done.other
  27.5 0.0 copy-start
  27.5 0.0 copy-start.1
  27.5 0.0 copy-start.2
  27.5 26.9 %ladder.1 = bf16[4,640,128]{2,1,0:T(8,128)(2,1)} custom-call(s32[5,1,8]{2,1,0:T(1,128)} %bitcast.15, bf16[4,640,128]{2,1,0:T(8,128)(2,1)S(1)} %bitcast.11, bf16[10,640,640]{2,1,0:T(8,128)(2,1)} %own.1, bf16[10,640,640]{2,1,0:T(8,128)(2,1)} %collective-permute-done.other), custom_call_target="tpu_custom_call" | custom-call | flops 16999999488 | bytes 20000000 | tf_op jit(solution)/shard_map/ladder/pallas_call | solution.py:212
  54.4 4.8 %all-to-all-start.1 = ((bf16[64,40,128]{2,1,0:T(8,128)(2,1)}), bf16[64,40,128]{2,1,0:T(8,128)(2,1)S(1)}, u32[]{:S(2)}, u32[]{:S(2)}) async-start(bf16[64,40,128]{2,1,0:T(8,128)(2,1)} %bitcast.3), calls=%async_computation.1 | async-start | bytes 1310720 | tf_op jit(solution)/shard_map/all_to_all | solution.py:245
  59.2 0.1 collective-permute-start.1
  59.3 1.2 %collective-permute-done.1.other_side = bf16[4,40,128]{2,1,0:T(8,128)(2,1)S(1)} collective-permute-done((bf16[4,40,128]{2,1,0:T(8,128)(2,1)S(1)}, bf16[4,40,128]{2,1,0:T(8,128)(2,1)S(1)}, u32[]{:S(2)}, u32[]{:S(2)}) %collective-permute-start.1) | collective-permute-done | bytes 40992 | tf_op jit(solution)/shard_map/ppermute | solution.py:232
  60.5 0.0 copy-done
  60.5 0.0 copy-done.1
  60.5 0.0 copy-done.2
  60.5 0.9 %local_terms.1 = (f32[40,128]{1,0:T(8,128)S(1)}, s32[40,128]{1,0:T(8,128)S(1)}) custom-call(s32[5,1,8]{2,1,0:T(1,128)S(1)} %bitcast.16, f32[8,8]{1,0:T(8,128)S(1)} %copy-done.2, bf16[4,40,128]{2,1,0:T(8,128)(2,1)S(1)} %dynamic-slice_bitcast_fusion.own_side, bf16[4,40,128]{2,1,0:T(8,128)(2,1)S(1)} %collective-permute-done.1.other_side, ...), custom_call_target="tpu_custom_call" | custom-call | tf_op jit(solution)/shard_map/local_terms/pallas_call | solution.py:233
  61.4 10.3 %all-to-all-done.1.sums = bf16[64,40,128]{2,1,0:T(8,128)(2,1)S(1)} async-done(((bf16[64,40,128]{2,1,0:T(8,128)(2,1)}), bf16[64,40,128]{2,1,0:T(8,128)(2,1)S(1)}, u32[]{:S(2)}, u32[]{:S(2)}) %all-to-all-start.1) | async-done | bytes 655392 | tf_op jit(solution)/shard_map/all_to_all | solution.py:245
  71.7 0.8 %final.1 = f32[40,1,640]{2,1,0:T(1,128)} custom-call(bf16[64,40,128]{2,1,0:T(8,128)(2,1)S(1)} %all-to-all-done.1.sums, f32[40,128]{1,0:T(8,128)S(1)} %get-tuple-element.7.local, s32[40,128]{1,0:T(8,128)S(1)} %get-tuple-element.8.tile_of_row), custom_call_target="tpu_custom_call" | custom-call | tf_op jit(solution)/shard_map/final/pallas_call | solution.py:246
  (1 shorter events, 0.0 us)
Async XLA Ops:
  0.0 27.5 %collective-permute-start = (bf16[10,640,640]{2,1,0:T(8,128)(2,1)}, bf16[10,640,640]{2,1,0:T(8,128)(2,1)}, u32[]{:S(2)}, u32[]{:S(2)}) collective-permute-start(bf16[10,640,640]{2,1,0:T(8,128)(2,1)} %own.1), channel_id=1, source_target_pairs={{0,16},{16,0},{1,17},{17,1},{2,18},{18,2},{3,19},{19,3},{4,20},{20... | collective-permute-start | bytes 24576008 | tf_op jit(solution)/shard_map/ppermute | solution.py:200
  27.5 33.0 %copy-start = (bf16[640,640]{1,0:T(8,128)(2,1)S(1)}, bf16[640,640]{1,0:T(8,128)(2,1)}, u32[]{:S(2)}) copy-start(bf16[640,640]{1,0:T(8,128)(2,1)} %fock.1) | copy-start | bytes 2457604
  27.5 33.0 %copy-start.1 = (s32[8,5,1]{0,2,1:T(1,128)S(1)}, s32[8,5,1]{0,2,1:T(1,128)}, u32[]{:S(2)}) copy-start(s32[8,5,1]{0,2,1:T(1,128)} %param.6) | copy-start | bytes 484
  27.5 33.0 %copy-start.2 = (f32[8,8]{1,0:T(8,128)S(1)}, f32[8,8]{1,0:T(8,128)}, u32[]{:S(2)}) copy-start(f32[8,8]{1,0:T(8,128)} %coupling.1) | copy-start | bytes 772
  54.4 17.3 %all-to-all-start.1 = ((bf16[64,40,128]{2,1,0:T(8,128)(2,1)}), bf16[64,40,128]{2,1,0:T(8,128)(2,1)S(1)}, u32[]{:S(2)}, u32[]{:S(2)}) async-start(bf16[64,40,128]{2,1,0:T(8,128)(2,1)} %bitcast.3), calls=%async_computation.1 | async-start | bytes 1310720 | tf_op jit(solution)/shard_map/all_to_all | solution.py:245
  59.2 1.3 %collective-permute-start.1 = (bf16[4,40,128]{2,1,0:T(8,128)(2,1)S(1)}, bf16[4,40,128]{2,1,0:T(8,128)(2,1)S(1)}, u32[]{:S(2)}, u32[]{:S(2)}) collective-permute-start(bf16[4,40,128]{2,1,0:T(8,128)(2,1)S(1)} %dynamic-slice_bitcast_fusion.own_side), channel_id=1, source_target_pairs={{0,16},{16,0},{1,17},{17,1},{2,18},{18,2},{3,19},{19,3},{4,20},{20... | collective-permute-start | bytes 122888 | tf_op jit(solution)/shard_map/ppermute | solution.py:232

commit v4 on v3

--- a/solution.py
+++ b/solution.py
@@ -42,7 +42,7 @@
     out[...] = jnp.broadcast_to(kept.astype(BF16)[None], out.shape)
 
 
-def ladder_kernel(lists_in, amps, own, other, out, lists, factor, half, sums, items, sems, list_sem):
+def ladder_kernel(lists_in, amps, own, other, out, lists, factor, half, sums, sent, items, sems, list_sem, out_sems):
     core = lax.axis_index("core")
     pairs, tiles = amps.shape[0], lists.shape[0]
     depth = own.shape[0]
@@ -66,7 +66,6 @@
                 need = need | (lists[row, 0, 2 * pair + core] == tile)
             items[count] = jnp.int32(pair * 8 + tile)
             count = count + need.astype(jnp.int32)
-    sums[...] = jnp.zeros_like(sums)
 
     def half_of(chunk, index):
         item = items[index]
@@ -119,19 +118,34 @@
             for tile in range(tiles):
                 copy(other, 1, tile).start()
 
-        for tile_a in range(tiles):
-            a_rows = pl.ds(tile_a * TILE, TILE)
-            left = jnp.concatenate([factor[chunk, level, a_rows, :] for level in range(depth)], axis=1)
-            right = jnp.concatenate(
-                [half[pair * tiles + lists[tile_a, 0, 2 * pair + core]] for pair in range(pairs)], axis=1
-            )
-            result = jnp.dot(left, right, preferred_element_type=F32)
-            for pair in range(pairs):
-                sums[pair, a_rows, :] += result[:, pair * TILE : (pair + 1) * TILE]
+        @pl.when(chunk == 0)
+        def _():
+            for tile_a in range(tiles):
+                for pair, (a_rows, value) in enumerate(products(0, tile_a)):
+                    sums[pair, a_rows, :] = value
+
         return carry
 
+    def products(chunk, tile_a):
+        a_rows = pl.ds(tile_a * TILE, TILE)
+        left = jnp.concatenate([factor[chunk, level, a_rows, :] for level in range(depth)], axis=1)
+        right = jnp.concatenate(
+            [half[pair * tiles + lists[tile_a, 0, 2 * pair + core]] for pair in range(pairs)], axis=1
+        )
+        result = jnp.dot(left, right, preferred_element_type=F32)
+        return [(a_rows, result[:, pair * TILE : (pair + 1) * TILE]) for pair in range(pairs)]
+
+    def send(tile):
+        a_rows = pl.ds(tile * TILE, TILE)
+        return pltpu.make_async_copy(sent.at[:, a_rows, :], out.at[:, a_rows, :], out_sems.at[tile])
+
     lax.fori_loop(0, 2, one_chunk, 0)
-    out[...] = sums[...].astype(BF16)
+    for tile_a in range(tiles):
+        for pair, (a_rows, value) in enumerate(products(1, tile_a)):
+            sent[pair, a_rows, :] = (sums[pair, a_rows, :] + value).astype(BF16)
+        send(tile_a).start()
+    for tile_a in range(tiles):
+        send(tile_a).wait()
 
 
 def local_kernel(lists, coupling, own_side, other_side, amps, fock_rows, fock, out, tile_of_row):
@@ -212,16 +226,18 @@
     partial_sums = pl.pallas_call(
         ladder_kernel,
         in_specs=[ANY, VMEM, ANY, ANY],
-        out_specs=VMEM,
-        out_shape=pltpu.VMEM((pairs, width, TILE), BF16),
+        out_specs=ANY,
+        out_shape=jax.ShapeDtypeStruct((pairs, width, TILE), BF16),
         scratch_shapes=[
             pltpu.SMEM(lists.shape, jnp.int32),
             pltpu.VMEM((2, depth, width, width), BF16),
             pltpu.VMEM((pairs * tiles, depth * width, TILE), BF16),
             pltpu.VMEM((pairs, width, TILE), F32),
+            pltpu.VMEM((pairs, width, TILE), BF16),
             pltpu.SMEM((pairs * tiles + 1,), jnp.int32),
             pltpu.SemaphoreType.DMA((2, tiles)),
             pltpu.SemaphoreType.DMA,
+            pltpu.SemaphoreType.DMA((tiles,)),
         ],
         compiler_params=pltpu.CompilerParams(vmem_limit_bytes=LADDER_VMEM),
         cost_estimate=pl.CostEstimate(flops=17 * 10**9, bytes_accessed=20 * 10**6, transcendentals=0),

time: 71.5 us -> 70.2 us (0.982); the launches traced: 72.5 us -> 69.9 us
  Pallas kernels: 29.4 us -> 26.2 us
    pallas_call x1, Pallas kernels: 26.9 us -> 23.7 us  [shards(): pl.pallas_call(ladder_kernel, in_specs=[ANY, VMEM, ANY, ANY], out_specs=A...]
  transfers between devices with their start and end apart: 3 -> 3, of which waited for: 2 -> 2; matrix products, arithmetic and copies ran while one was open for 0% -> 0% of each run, Pallas kernels for 2% -> 3%
where the time goes in v4:
time: 70.2 us; the launch traced here: 69.9 us
  blocking collectives  26.6 us (38%)
  Pallas kernels  26.2 us (37%)
  waiting for transfers between devices  12.1 us (17%)
  starting transfers between devices  4.87 us (7%)
    all_to_all x1, blocking collectives, shards(): gathered = lax.all_to_all(repeated, SAME_CORE, 0, 0, tiled=True)  26.6 us
    pallas_call x1, Pallas kernels, shards(): pl.pallas_call(ladder_kernel, in_specs=[ANY, VMEM, ANY, ANY], out_specs=A...  23.7 us
    all_to_all x1, waiting for transfers between devices, shards(): lax.all_to_all(partial_sums.reshape(peers, rows, TILE), SAME_CORE, 0, 0,...  10.9 us
    all_to_all x1, starting transfers between devices, shards(): lax.all_to_all(partial_sums.reshape(peers, rows, TILE), SAME_CORE, 0, 0,...  4.78 us
  transfers between devices with their start and end apart: 3, of which 2 were waited for; matrix products, arithmetic and copies ran while one was open for 0% of the time, Pallas kernels for 3%

profile of v4, /device:TPU:0, one launch (start us, length us, event | category | flops | bytes accessed | tf_op | source)
XLA Modules:
  0.0 69.9 jit_solution(16370765198749485630)
XLA Ops:
  0.0 0.0 collective-permute-start
  0.0 0.9 %compact.1 = bf16[64,40,128]{2,1,0:T(8,128)(2,1)S(1)} custom-call(s32[5,1,8]{2,1,0:T(1,128)} %bitcast.14, bf16[40,640]{1,0:T(8,128)(2,1)} %bitcast.18), custom_call_target="tpu_custom_call" | custom-call | tf_op jit(solution)/shard_map/compact/pallas_call | solution.py:215
  0.9 26.6 %all_to_all.10 = bf16[64,40,128]{2,1,0:T(8,128)(2,1)S(1)} all-to-all(bf16[64,40,128]{2,1,0:T(8,128)(2,1)S(1)} %compact.1), channel_id=1, replica_groups=mesh['z'=4,'core'=2,'x'=4,'y'=4] {'z','x','y'}, dimensions={0} | all-to-all | bytes 1310720 | tf_op jit(solution)/shard_map/all_to_all | solution.py:223
  27.5 0.0 collective-permute-done.other
  27.5 0.0 copy-start
  27.5 0.0 copy-start.1
  27.5 0.0 copy-start.2
  27.5 23.7 %ladder.1 = bf16[4,640,128]{2,1,0:T(8,128)(2,1)} custom-call(s32[5,1,8]{2,1,0:T(1,128)} %bitcast.15, bf16[4,640,128]{2,1,0:T(8,128)(2,1)S(1)} %bitcast.11, bf16[10,640,640]{2,1,0:T(8,128)(2,1)} %own.1, bf16[10,640,640]{2,1,0:T(8,128)(2,1)} %collective-permute-done.other), custom_call_target="tpu_custom_call" | custom-call | flops 16999999488 | bytes 20000000 | tf_op jit(solution)/shard_map/ladder/pallas_call | solution.py:226
  51.2 4.8 %all-to-all-start.1 = ((bf16[64,40,128]{2,1,0:T(8,128)(2,1)}), bf16[64,40,128]{2,1,0:T(8,128)(2,1)S(1)}, u32[]{:S(2)}, u32[]{:S(2)}) async-start(bf16[64,40,128]{2,1,0:T(8,128)(2,1)} %bitcast.17), calls=%async_computation.1 | async-start | bytes 1310720 | tf_op jit(solution)/shard_map/all_to_all | solution.py:261
  56.0 0.1 collective-permute-start.1
  56.1 1.2 %collective-permute-done.1.other_side = bf16[4,40,128]{2,1,0:T(8,128)(2,1)S(1)} collective-permute-done((bf16[4,40,128]{2,1,0:T(8,128)(2,1)S(1)}, bf16[4,40,128]{2,1,0:T(8,128)(2,1)S(1)}, u32[]{:S(2)}, u32[]{:S(2)}) %collective-permute-start.1) | collective-permute-done | bytes 40992 | tf_op jit(solution)/shard_map/ppermute | solution.py:248
  57.3 0.0 copy-done
  57.3 0.0 copy-done.1
  57.3 0.0 copy-done.2
  57.3 0.9 %local_terms.1 = (f32[40,128]{1,0:T(8,128)S(1)}, s32[40,128]{1,0:T(8,128)S(1)}) custom-call(s32[5,1,8]{2,1,0:T(1,128)S(1)} %bitcast.16, f32[8,8]{1,0:T(8,128)S(1)} %copy-done.2, bf16[4,40,128]{2,1,0:T(8,128)(2,1)S(1)} %dynamic-slice_bitcast_fusion.own_side, bf16[4,40,128]{2,1,0:T(8,128)(2,1)S(1)} %collective-permute-done.1.other_side, ...), custom_call_target="tpu_custom_call" | custom-call | tf_op jit(solution)/shard_map/local_terms/pallas_call | solution.py:249
  58.2 10.9 %all-to-all-done.1.sums = bf16[64,40,128]{2,1,0:T(8,128)(2,1)S(1)} async-done(((bf16[64,40,128]{2,1,0:T(8,128)(2,1)}), bf16[64,40,128]{2,1,0:T(8,128)(2,1)S(1)}, u32[]{:S(2)}, u32[]{:S(2)}) %all-to-all-start.1) | async-done | bytes 655392 | tf_op jit(solution)/shard_map/all_to_all | solution.py:261
  69.1 0.8 %final.1 = f32[40,1,640]{2,1,0:T(1,128)} custom-call(bf16[64,40,128]{2,1,0:T(8,128)(2,1)S(1)} %all-to-all-done.1.sums, f32[40,128]{1,0:T(8,128)S(1)} %get-tuple-element.7.local, s32[40,128]{1,0:T(8,128)S(1)} %get-tuple-element.8.tile_of_row), custom_call_target="tpu_custom_call" | custom-call | tf_op jit(solution)/shard_map/final/pallas_call | solution.py:262
  (1 shorter events, 0.0 us)
Async XLA Ops:
  0.0 27.5 %collective-permute-start = (bf16[10,640,640]{2,1,0:T(8,128)(2,1)}, bf16[10,640,640]{2,1,0:T(8,128)(2,1)}, u32[]{:S(2)}, u32[]{:S(2)}) collective-permute-start(bf16[10,640,640]{2,1,0:T(8,128)(2,1)} %own.1), channel_id=1, source_target_pairs={{0,16},{16,0},{1,17},{17,1},{2,18},{18,2},{3,19},{19,3},{4,20},{20... | collective-permute-start | bytes 24576008 | tf_op jit(solution)/shard_map/ppermute | solution.py:214
  27.5 29.8 %copy-start = (bf16[640,640]{1,0:T(8,128)(2,1)S(1)}, bf16[640,640]{1,0:T(8,128)(2,1)}, u32[]{:S(2)}) copy-start(bf16[640,640]{1,0:T(8,128)(2,1)} %fock.1) | copy-start | bytes 2457604
  27.5 29.8 %copy-start.1 = (s32[8,5,1]{0,2,1:T(1,128)S(1)}, s32[8,5,1]{0,2,1:T(1,128)}, u32[]{:S(2)}) copy-start(s32[8,5,1]{0,2,1:T(1,128)} %param.6) | copy-start | bytes 484
  27.5 29.8 %copy-start.2 = (f32[8,8]{1,0:T(8,128)S(1)}, f32[8,8]{1,0:T(8,128)}, u32[]{:S(2)}) copy-start(f32[8,8]{1,0:T(8,128)} %coupling.1) | copy-start | bytes 772
  51.2 17.9 %all-to-all-start.1 = ((bf16[64,40,128]{2,1,0:T(8,128)(2,1)}), bf16[64,40,128]{2,1,0:T(8,128)(2,1)S(1)}, u32[]{:S(2)}, u32[]{:S(2)}) async-start(bf16[64,40,128]{2,1,0:T(8,128)(2,1)} %bitcast.17), calls=%async_computation.1 | async-start | bytes 1310720 | tf_op jit(solution)/shard_map/all_to_all | solution.py:261
  56.0 1.3 %collective-permute-start.1 = (bf16[4,40,128]{2,1,0:T(8,128)(2,1)S(1)}, bf16[4,40,128]{2,1,0:T(8,128)(2,1)S(1)}, u32[]{:S(2)}, u32[]{:S(2)}) collective-permute-start(bf16[4,40,128]{2,1,0:T(8,128)(2,1)S(1)} %dynamic-slice_bitcast_fusion.own_side), channel_id=1, source_target_pairs={{0,16},{16,0},{1,17},{17,1},{2,18},{18,2},{3,19},{19,3},{4,20},{20... | collective-permute-start | bytes 122888 | tf_op jit(solution)/shard_map/ppermute | solution.py:248

commit v5 on v4

--- a/solution.py
+++ b/solution.py
@@ -58,6 +58,8 @@
             list_copy = pltpu.make_async_copy(lists_in, lists, list_sem)
             list_copy.start()
     list_copy.wait()
+    for tile in range(tiles):
+        copy(other, 1, tile).start()
     count = jnp.int32(0)
     for tile in range(tiles):
         for pair in range(pairs):
@@ -112,11 +114,6 @@
             0, count // AT_ONCE, lambda step, seen: several(first + step * AT_ONCE, AT_ONCE, seen), arrived
         )
         wait_up_to(chunk, arrived, jnp.int32(tiles - 1))
-
-        @pl.when(chunk == 0)
-        def _():
-            for tile in range(tiles):
-                copy(other, 1, tile).start()
 
         @pl.when(chunk == 0)
         def _():

time: 70.2 us -> 70.5 us (level); the launches traced: 69.9 us -> 69.2 us
  Pallas kernels: 26.2 us -> 25 us
    pallas_call x1, Pallas kernels: 23.7 us -> 22.4 us  [shards(): pl.pallas_call(ladder_kernel, in_specs=[ANY, VMEM, ANY, ANY], out_specs=A...]
where the time goes in v5:
time: 70.5 us; the launch traced here: 69.2 us
  blocking collectives  26.6 us (38%)
  Pallas kernels  25 us (35%)
  waiting for transfers between devices  12.6 us (18%)
  starting transfers between devices  4.87 us (7%)
    all_to_all x1, blocking collectives, shards(): gathered = lax.all_to_all(repeated, SAME_CORE, 0, 0, tiled=True)  26.6 us
    pallas_call x1, Pallas kernels, shards(): pl.pallas_call(ladder_kernel, in_specs=[ANY, VMEM, ANY, ANY], out_specs=A...  22.4 us
    all_to_all x1, waiting for transfers between devices, shards(): lax.all_to_all(partial_sums.reshape(peers, rows, TILE), SAME_CORE, 0, 0,...  11.4 us
    all_to_all x1, starting transfers between devices, shards(): lax.all_to_all(partial_sums.reshape(peers, rows, TILE), SAME_CORE, 0, 0,...  4.78 us
  transfers between devices with their start and end apart: 3, of which 2 were waited for; matrix products, arithmetic and copies ran while one was open for 0% of the time, Pallas kernels for 3%

profile of v5, /device:TPU:0, one launch (start us, length us, event | category | flops | bytes accessed | tf_op | source)
XLA Modules:
  0.0 69.2 jit_solution(11159800141350391642)
XLA Ops:
  0.0 0.0 collective-permute-start
  0.0 0.9 %compact.1 = bf16[64,40,128]{2,1,0:T(8,128)(2,1)S(1)} custom-call(s32[5,1,8]{2,1,0:T(1,128)} %bitcast.14, bf16[40,640]{1,0:T(8,128)(2,1)} %bitcast.18), custom_call_target="tpu_custom_call" | custom-call | tf_op jit(solution)/shard_map/compact/pallas_call | solution.py:212
  0.9 26.6 %all_to_all.10 = bf16[64,40,128]{2,1,0:T(8,128)(2,1)S(1)} all-to-all(bf16[64,40,128]{2,1,0:T(8,128)(2,1)S(1)} %compact.1), channel_id=1, replica_groups=mesh['z'=4,'core'=2,'x'=4,'y'=4] {'z','x','y'}, dimensions={0} | all-to-all | bytes 1310720 | tf_op jit(solution)/shard_map/all_to_all | solution.py:220
  27.5 0.0 collective-permute-done.other
  27.5 0.0 copy-start
  27.5 0.0 copy-start.1
  27.5 0.0 copy-start.2
  27.5 22.4 %ladder.1 = bf16[4,640,128]{2,1,0:T(8,128)(2,1)} custom-call(s32[5,1,8]{2,1,0:T(1,128)} %bitcast.15, bf16[4,640,128]{2,1,0:T(8,128)(2,1)S(1)} %bitcast.11, bf16[10,640,640]{2,1,0:T(8,128)(2,1)} %own.1, bf16[10,640,640]{2,1,0:T(8,128)(2,1)} %collective-permute-done.other), custom_call_target="tpu_custom_call" | custom-call | flops 16999999488 | bytes 20000000 | tf_op jit(solution)/shard_map/ladder/pallas_call | solution.py:223
  49.9 4.8 %all-to-all-start.1 = ((bf16[64,40,128]{2,1,0:T(8,128)(2,1)}), bf16[64,40,128]{2,1,0:T(8,128)(2,1)S(1)}, u32[]{:S(2)}, u32[]{:S(2)}) async-start(bf16[64,40,128]{2,1,0:T(8,128)(2,1)} %bitcast.17), calls=%async_computation.1 | async-start | bytes 1310720 | tf_op jit(solution)/shard_map/all_to_all | solution.py:258
  54.8 0.1 collective-permute-start.1
  54.8 1.2 %collective-permute-done.1.other_side = bf16[4,40,128]{2,1,0:T(8,128)(2,1)S(1)} collective-permute-done((bf16[4,40,128]{2,1,0:T(8,128)(2,1)S(1)}, bf16[4,40,128]{2,1,0:T(8,128)(2,1)S(1)}, u32[]{:S(2)}, u32[]{:S(2)}) %collective-permute-start.1) | collective-permute-done | bytes 40992 | tf_op jit(solution)/shard_map/ppermute | solution.py:245
  56.1 0.0 copy-done
  56.1 0.0 copy-done.1
  56.1 0.0 copy-done.2
  56.1 0.9 %local_terms.1 = (f32[40,128]{1,0:T(8,128)S(1)}, s32[40,128]{1,0:T(8,128)S(1)}) custom-call(s32[5,1,8]{2,1,0:T(1,128)S(1)} %bitcast.16, f32[8,8]{1,0:T(8,128)S(1)} %copy-done.2, bf16[4,40,128]{2,1,0:T(8,128)(2,1)S(1)} %dynamic-slice_bitcast_fusion.own_side, bf16[4,40,128]{2,1,0:T(8,128)(2,1)S(1)} %collective-permute-done.1.other_side, ...), custom_call_target="tpu_custom_call" | custom-call | tf_op jit(solution)/shard_map/local_terms/pallas_call | solution.py:246
  56.9 11.4 %all-to-all-done.1.sums = bf16[64,40,128]{2,1,0:T(8,128)(2,1)S(1)} async-done(((bf16[64,40,128]{2,1,0:T(8,128)(2,1)}), bf16[64,40,128]{2,1,0:T(8,128)(2,1)S(1)}, u32[]{:S(2)}, u32[]{:S(2)}) %all-to-all-start.1) | async-done | bytes 655392 | tf_op jit(solution)/shard_map/all_to_all | solution.py:258
  68.4 0.8 %final.1 = f32[40,1,640]{2,1,0:T(1,128)} custom-call(bf16[64,40,128]{2,1,0:T(8,128)(2,1)S(1)} %all-to-all-done.1.sums, f32[40,128]{1,0:T(8,128)S(1)} %get-tuple-element.7.local, s32[40,128]{1,0:T(8,128)S(1)} %get-tuple-element.8.tile_of_row), custom_call_target="tpu_custom_call" | custom-call | tf_op jit(solution)/shard_map/final/pallas_call | solution.py:259
  (1 shorter events, 0.0 us)
Async XLA Ops:
  0.0 27.5 %collective-permute-start = (bf16[10,640,640]{2,1,0:T(8,128)(2,1)}, bf16[10,640,640]{2,1,0:T(8,128)(2,1)}, u32[]{:S(2)}, u32[]{:S(2)}) collective-permute-start(bf16[10,640,640]{2,1,0:T(8,128)(2,1)} %own.1), channel_id=1, source_target_pairs={{0,16},{16,0},{1,17},{17,1},{2,18},{18,2},{3,19},{19,3},{4,20},{20... | collective-permute-start | bytes 24576008 | tf_op jit(solution)/shard_map/ppermute | solution.py:211
  27.5 28.6 %copy-start = (bf16[640,640]{1,0:T(8,128)(2,1)S(1)}, bf16[640,640]{1,0:T(8,128)(2,1)}, u32[]{:S(2)}) copy-start(bf16[640,640]{1,0:T(8,128)(2,1)} %fock.1) | copy-start | bytes 2457604
  27.5 28.6 %copy-start.1 = (s32[8,5,1]{0,2,1:T(1,128)S(1)}, s32[8,5,1]{0,2,1:T(1,128)}, u32[]{:S(2)}) copy-start(s32[8,5,1]{0,2,1:T(1,128)} %param.6) | copy-start | bytes 484
  27.5 28.6 %copy-start.2 = (f32[8,8]{1,0:T(8,128)S(1)}, f32[8,8]{1,0:T(8,128)}, u32[]{:S(2)}) copy-start(f32[8,8]{1,0:T(8,128)} %coupling.1) | copy-start | bytes 772
  49.9 18.4 %all-to-all-start.1 = ((bf16[64,40,128]{2,1,0:T(8,128)(2,1)}), bf16[64,40,128]{2,1,0:T(8,128)(2,1)S(1)}, u32[]{:S(2)}, u32[]{:S(2)}) async-start(bf16[64,40,128]{2,1,0:T(8,128)(2,1)} %bitcast.17), calls=%async_computation.1 | async-start | bytes 1310720 | tf_op jit(solution)/shard_map/all_to_all | solution.py:258
  54.8 1.3 %collective-permute-start.1 = (bf16[4,40,128]{2,1,0:T(8,128)(2,1)S(1)}, bf16[4,40,128]{2,1,0:T(8,128)(2,1)S(1)}, u32[]{:S(2)}, u32[]{:S(2)}) collective-permute-start(bf16[4,40,128]{2,1,0:T(8,128)(2,1)S(1)} %dynamic-slice_bitcast_fusion.own_side), channel_id=1, source_target_pairs={{0,16},{16,0},{1,17},{17,1},{2,18},{18,2},{3,19},{19,3},{4,20},{20... | collective-permute-start | bytes 122888 | tf_op jit(solution)/shard_map/ppermute | solution.py:245
